TPU v7x, 256 devices: a whole 4x4x8 slice. The times are simulated.
256 devices in a mesh: gx: 8 (over x, core), gy: 32 (over z, y).
Axes of the slice: x: 4, y: 4, z: 8, core: 2. Of those that a mesh axis runs over, the one named last changes fastest.
Arguments:
- state_field: float32 [256, 512, 16, 256], P('gx', 'gy'), may hold values from -80 to 80
- start_basis: float32 [256, 32], replicated, may hold values from -6 to 6
Outputs:
- core_tensor: float32 [256, 512, 512], P('gx', 'gy')
- z_factor: float32 [256, 32], replicated
- x_triangle: float32 [256, 256], replicated
All inputs are finite; a program needn't handle non-finite values.
Results may differ from a plain program's by a relative error of at most 0.0003.
Values sent between devices are 32-bit elements; how exact they have to be, the bound alone decides.
A program may use at most 64 MiB of HBM per device.

v0:
```python
import jax
import jax.numpy as jnp
from jax import lax
from jax.sharding import PartitionSpec as P

ITERS = 3
precise = lax.Precision.HIGHEST


def orthonormal(image):
    for repeat in range(2):
        inner_gram = jnp.dot(image.T, image, precision=precise, preferred_element_type=jnp.float32)
        lower_factor = jnp.linalg.cholesky(inner_gram)
        image = lax.linalg.triangular_solve(
            lower_factor, image, left_side=False, lower=True, transpose_a=True
        )
    return image


def local(state_field, start_basis):
    x_cells, y_cells, species, z_cells = state_field.shape
    unfolded = state_field.reshape(x_cells * y_cells * species, z_cells)
    local_gram = lax.dot_general(
        unfolded,
        unfolded,
        (((0,), (0,)), ((), ())),
        precision=precise,
        preferred_element_type=jnp.float32,
    )
    z_basis = start_basis
    gram_z = lax.psum(local_gram, ("gx", "gy"))
    for iteration in range(ITERS):
        z_basis = orthonormal(
            jnp.dot(gram_z, z_basis, precision=precise, preferred_element_type=jnp.float32)
        )
    rank_kept = z_basis.shape[1]
    core_rows = jnp.dot(unfolded, z_basis, precision=precise, preferred_element_type=jnp.float32)
    core_tensor = core_rows.reshape(x_cells, y_cells, species * rank_kept)
    x_total = x_cells * lax.axis_size("gx")
    regrouped = lax.all_to_all(core_tensor, "gx", split_axis=2, concat_axis=0, tiled=True)
    x_rows = regrouped.reshape(x_total, -1)
    local_xgram = jnp.dot(x_rows, x_rows.T, precision=precise, preferred_element_type=jnp.float32)
    gram_x = lax.psum(local_xgram, ("gx", "gy"))
    column_count = y_cells * lax.axis_size("gy") * species * rank_kept
    x_triangle = jnp.linalg.cholesky(gram_x).T / jnp.sqrt(jnp.float32(column_count))
    return (core_tensor, z_basis, x_triangle)


def solution(mesh):
    return jax.shard_map(
        local,
        mesh=mesh,
        in_specs=(P("gx", "gy", None, None), P()),
        out_specs=(P("gx", "gy", None), P(), P()),
        check_vma=False,
    )
```

profile of v0, /device:TPU:2, one launch (start us, length us, event | category | flops | bytes accessed | tf_op | source)
XLA Modules:
  0.0 675.3 jit_solution(2987790697292606197)
XLA Ops:
  7.2 17.8 %convolution_bitcast_fusion.1 = f32[256,256]{1,0:T(8,128)} fusion(f32[32,16,16,256]{3,2,1,0:T(8,128)} %param.5), kind=kOutput, calls=%fused_computation.1 | convolution fusion | flops 6442450944 | bytes 8650752 | tf_op jit(solution)/shard_map/dot_general | solution.py:23
  25.3 253.2 %all-reduce.4.cloned.1.call-done = f32[256,256]{1,0:T(8,128)} async-done(((f32[256,256]{1,0:T(8,128)}), f32[256,256]{1,0:T(8,128)}) %all-reduce.4.cloned.1.call-update) | async-done | bytes 262160 | tf_op jit(solution)/shard_map/psum | solution.py:31
  278.4 1.3 fusion.32
  280.0 2.9 cholesky.222
  282.9 0.6 compare_reduce_fusion.5
  283.6 0.7 fusion.4
  284.2 2.4 custom-call.22
  287.2 2.9 cholesky.233
  290.1 0.6 compare_reduce_fusion.4
  290.8 0.7 fusion.5
  291.4 2.4 custom-call.23
  294.1 1.3 fusion.35
  295.7 2.9 cholesky.244
  298.6 0.6 compare_reduce_fusion.3
  299.3 0.7 fusion.6
  299.9 2.4 custom-call.24
  302.9 2.9 cholesky.255
  305.8 0.6 compare_reduce_fusion.2
  306.5 0.7 fusion.7
  307.1 2.4 custom-call.25
  309.8 1.3 fusion.38
  311.3 2.9 cholesky.266
  314.3 0.6 compare_reduce_fusion.1
  314.9 0.7 fusion.8
  315.6 2.4 custom-call.26
  318.5 2.9 cholesky.277
  321.5 0.6 compare_reduce_fusion
  322.1 0.7 fusion.9
  322.8 2.4 custom-call.27
  325.5 9.9 %convolution_bitcast_fusion = f32[8192,32]{0,1:T(8,128)S(1)} fusion(f32[256,32]{0,1:T(8,128)S(1)} %convolution_bitcast_fusion.2, f32[8192,256]{1,0:T(8,128)} %bitcast.127), kind=kOutput, calls=%fused_computation | convolution fusion | flops 805306368 | bytes 9469952 | tf_op jit(solution)/shard_map/dot_general | solution.py:37
  335.4 2.6 copy.47
  338.0 3.5 reshape.41
  341.6 3.8 copy.48
  345.4 3.9 reshape.66
  349.3 19.2 %all_to_all.15 = f32[8,1,32768]{2,1,0:T(1,128)S(1)} all-to-all(f32[8,1,32768]{2,1,0:T(1,128)S(1)} %reshape.66), channel_id=1, replica_groups=mesh['gx'=8,'gy'=32] {'gx'}, dimensions={0} | all-to-all | bytes 2097152 | tf_op jit(solution)/shard_map/all_to_all | solution.py:40
  369.1 3.1 reduce.16
  372.2 3.3 reshape.67
  375.5 3.6 copy.49
  379.2 0.6 reshape.42
  379.7 1.7 fusion.41
  381.5 248.1 %all-reduce.6.cloned.1.call-done = f32[256,256]{0,1:T(8,128)} async-done(((f32[256,256]{0,1:T(8,128)}), f32[256,256]{0,1:T(8,128)}) %all-reduce.6.cloned.1.call-update) | async-done | bytes 262160 | tf_op jit(solution)/shard_map/psum | solution.py:43
  629.6 1.1 copy.51
  630.7 1.0 fusion
  631.7 11.7 %cholesky.77 = f32[128,128]{1,0:T(8,128)S(1)} custom-call(f32[128,128]{1,0:T(8,128)S(1)} %cholesky.286), custom_call_target="Cholesky" | custom-call | tf_op jit(solution)/shard_map/jit(cholesky)/cholesky | solution.py:45
  643.4 9.8 %custom-call.16 = f32[1,128,128]{1,2,0:T(8,128)S(1)} custom-call(f32[1,128,128]{2,1,0:T(8,128)S(1)} %get-tuple-element.20), custom_call_target="InvertDiagBlocksLowerTriangular" | custom-call | tf_op jit(solution)/shard_map/jit(cholesky)/cholesky | solution.py:45
  653.8 11.7 %cholesky.132 = f32[128,128]{1,0:T(8,128)S(1)} custom-call(f32[128,128]{1,0:T(8,128)S(1)} %convolution_subtract_fusion), custom_call_target="Cholesky" | custom-call | tf_op jit(solution)/shard_map/jit(cholesky)/cholesky | solution.py:45
  665.5 0.7 compare_reduce_fusion.6
  667.6 0.8 copy.52
  (48 shorter events, 4.5 us)
Async XLA Ops:
  7.2 271.3 %copy-start = (f32[256,32]{0,1:T(8,128)S(1)}, f32[256,32]{0,1:T(8,128)}, u32[]{:S(2)}) copy-start(f32[256,32]{0,1:T(8,128)} %param.6) | copy-start | bytes 98308
  7.2 271.2 %all-reduce.4.cloned.1.call-start = ((), (), s32[]{:S(2)}) async-start(), calls=%async_computation.1 | async-start | bytes 524288 | tf_op jit(solution)/shard_map/psum | solution.py:31
  25.0 604.6 %all-reduce.6.cloned.1.call-start = ((), (), s32[]{:S(2)}) async-start(), calls=%async_computation.2 | async-start | bytes 524288 | tf_op jit(solution)/shard_map/psum | solution.py:43
  325.5 16.1 %copy-start.2 = (f32[256,32]{0,1:T(8,128)}, f32[256,32]{0,1:T(8,128)S(1)}, u32[]{:S(2)}) copy-start(f32[256,32]{0,1:T(8,128)S(1)} %convolution_bitcast_fusion.2) | copy-start | bytes 98308
  341.6 34.0 %copy-start.1 = (f32[32,16,512]{2,1,0:T(8,128)}, f32[32,16,512]{2,1,0:T(8,128)S(1)}, u32[]{:S(2)}) copy-start(f32[32,16,512]{2,1,0:T(8,128)S(1)} %reshape.41) | copy-start | bytes 3145732
Sparse Core Ops, SparseCore 0:
  25.2 253.2 all-reduce.3
  381.6 247.9 all-reduce.5
where the time goes:
time: 676 us; the launch traced here: 675 us
  waiting for transfers between devices  501 us (74%)
  other arithmetic  78.3 us (12%)
  matrix products  36.2 us (5%)
  local copies, waits for them, and re-layouts  24.3 us (4%)
  blocking collectives  19.2 us (3%)
  between operations  15.7 us (2%)
    psum x1, waiting for transfers between devices, local(): gram_z = lax.psum(local_gram, ('gx', 'gy'))  253 us
    psum x1, waiting for transfers between devices, local(): gram_x = lax.psum(local_xgram, ('gx', 'gy'))  248 us
    another operation x6, other arithmetic, local(): jnp.linalg.cholesky(gram_x).T / jnp.sqrt(jnp.float32(column_count))  34 us
    another operation x18, other arithmetic, orthonormal(): lower_factor = jnp.linalg.cholesky(inner_gram)  21.6 us
    all_to_all x1, blocking collectives, local(): lax.all_to_all(core_tensor, 'gx', split_axis=2, concat_axis=0, tiled=True)  19.2 us
    another operation x12, other arithmetic, orthonormal(): lax.linalg.triangular_solve(lower_factor, image, left_side=False, lower=T...  18.5 us
    dot_general x1, matrix products, local(): lax.dot_general(unfolded, unfolded, (((0,), (0,)), ((), ())), precision=p...  17.8 us
  transfers between devices with their start and end apart: 2, of which 2 were waited for; matrix products, arithmetic and copies ran while one was open for 0% of the time, Pallas kernels for 0%

commit v1 on v0

--- a/solution.py
+++ b/solution.py
@@ -28,7 +28,7 @@
         preferred_element_type=jnp.float32,
     )
     z_basis = start_basis
-    gram_z = lax.psum(local_gram, ("gx", "gy"))
+    gram_z = lax.psum(lax.psum(local_gram, "gy"), "gx")
     for iteration in range(ITERS):
         z_basis = orthonormal(
             jnp.dot(gram_z, z_basis, precision=precise, preferred_element_type=jnp.float32)

time: 676 us -> 635 us (0.939)
  waiting for transfers between devices: 501 us -> 460 us
    psum x1 -> x2, waiting for transfers between devices: 253 us -> 209 us  [local(): gram_z = lax.psum(lax.psum(local_gram, 'gy'), 'gx')]
  transfers between devices with their start and end apart: 2 -> 3, of which waited for: 2 -> 3; matrix products, arithmetic and copies ran while one was open for 0% -> 0% of each run, Pallas kernels for 0% -> 0%
where the time goes in v1:
time: 635 us; the launch traced here: 634 us
  waiting for transfers between devices  460 us (72%)
  other arithmetic  78.3 us (12%)
  matrix products  36.2 us (6%)
  local copies, waits for them, and re-layouts  24.3 us (4%)
  blocking collectives  19.8 us (3%)
  between operations  15.4 us (2%)
    psum x1, waiting for transfers between devices, local(): gram_x = lax.psum(local_xgram, ('gx', 'gy'))  251 us
    psum x2, waiting for transfers between devices, local(): gram_z = lax.psum(lax.psum(local_gram, 'gy'), 'gx')  209 us
    another operation x6, other arithmetic, local(): jnp.linalg.cholesky(gram_x).T / jnp.sqrt(jnp.float32(column_count))  34 us
    another operation x18, other arithmetic, orthonormal(): lower_factor = jnp.linalg.cholesky(inner_gram)  21.6 us
    all_to_all x1, blocking collectives, local(): lax.all_to_all(core_tensor, 'gx', split_axis=2, concat_axis=0, tiled=True)  19.8 us
    another operation x12, other arithmetic, orthonormal(): lax.linalg.triangular_solve(lower_factor, image, left_side=False, lower=T...  18.5 us
    dot_general x1, matrix products, local(): lax.dot_general(unfolded, unfolded, (((0,), (0,)), ((), ())), precision=p...  17.8 us
  transfers between devices with their start and end apart: 3, of which 3 were waited for; matrix products, arithmetic and copies ran while one was open for 0% of the time, Pallas kernels for 0%

profile of v1, /device:TPU:2, one launch (start us, length us, event | category | flops | bytes accessed | tf_op | source)
XLA Modules:
  0.0 634.2 jit_solution(4030045900289379664)
XLA Ops:
  7.2 17.8 %convolution_bitcast_fusion.1 = f32[256,256]{1,0:T(8,128)} fusion(f32[32,16,16,256]{3,2,1,0:T(8,128)} %param.5), kind=kOutput, calls=%fused_computation.1 | convolution fusion | flops 6442450944 | bytes 8650752 | tf_op jit(solution)/shard_map/dot_general | solution.py:23
  25.1 147.3 %all-reduce.5.cloned.1.call-done = f32[256,256]{1,0:T(8,128)} async-done(((f32[256,256]{1,0:T(8,128)}), f32[256,256]{1,0:T(8,128)}) %all-reduce.5.cloned.1.call-update) | async-done | bytes 262160 | tf_op jit(solution)/shard_map/psum | solution.py:31
  172.6 61.8 %all-reduce.7.cloned.1.call-done = f32[256,256]{1,0:T(8,128)} async-done(((f32[256,256]{1,0:T(8,128)}), f32[256,256]{1,0:T(8,128)}) %all-reduce.7.cloned.1.call-update) | async-done | bytes 262160 | tf_op jit(solution)/shard_map/psum | solution.py:31
  234.4 1.3 fusion.32
  235.9 2.9 cholesky.222
  238.9 0.6 compare_reduce_fusion.5
  239.5 0.7 fusion.4
  240.2 2.4 custom-call.22
  243.1 2.9 cholesky.233
  246.1 0.6 compare_reduce_fusion.4
  246.7 0.7 fusion.5
  247.4 2.4 custom-call.23
  250.1 1.3 fusion.35
  251.6 2.9 cholesky.244
  254.6 0.6 compare_reduce_fusion.3
  255.2 0.7 fusion.6
  255.9 2.4 custom-call.24
  258.8 2.9 cholesky.255
  261.8 0.6 compare_reduce_fusion.2
  262.4 0.7 fusion.7
  263.1 2.4 custom-call.25
  265.8 1.3 fusion.38
  267.3 2.9 cholesky.266
  270.3 0.6 compare_reduce_fusion.1
  270.9 0.7 fusion.8
  271.6 2.4 custom-call.26
  274.5 2.9 cholesky.277
  277.5 0.6 compare_reduce_fusion
  278.1 0.7 fusion.9
  278.8 2.4 custom-call.27
  281.5 9.9 %convolution_bitcast_fusion = f32[8192,32]{0,1:T(8,128)S(1)} fusion(f32[256,32]{0,1:T(8,128)S(1)} %convolution_bitcast_fusion.2, f32[8192,256]{1,0:T(8,128)} %bitcast.127), kind=kOutput, calls=%fused_computation | convolution fusion | flops 805306368 | bytes 9469952 | tf_op jit(solution)/shard_map/dot_general | solution.py:37
  291.3 2.6 copy.47
  294.0 3.5 reshape.41
  297.5 3.8 copy.48
  301.4 3.9 reshape.66
  305.3 19.8 %all_to_all.15 = f32[8,1,32768]{2,1,0:T(1,128)S(1)} all-to-all(f32[8,1,32768]{2,1,0:T(1,128)S(1)} %reshape.66), channel_id=1, replica_groups=mesh['gx'=8,'gy'=32] {'gx'}, dimensions={0} | all-to-all | bytes 2097152 | tf_op jit(solution)/shard_map/all_to_all | solution.py:40
  325.6 3.1 reduce.16
  328.7 3.3 reshape.67
  332.0 3.6 copy.49
  336.2 1.7 fusion.41
  338.0 250.8 %all-reduce.9.cloned.1.call-done = f32[256,256]{0,1:T(8,128)} async-done(((f32[256,256]{0,1:T(8,128)}), f32[256,256]{0,1:T(8,128)}) %all-reduce.9.cloned.1.call-update) | async-done | bytes 262160 | tf_op jit(solution)/shard_map/psum | solution.py:43
  588.8 1.1 copy.51
  589.9 1.0 fusion
  590.9 11.7 %cholesky.77 = f32[128,128]{1,0:T(8,128)S(1)} custom-call(f32[128,128]{1,0:T(8,128)S(1)} %cholesky.286), custom_call_target="Cholesky" | custom-call | tf_op jit(solution)/shard_map/jit(cholesky)/cholesky | solution.py:45
  602.6 9.8 %custom-call.16 = f32[1,128,128]{1,2,0:T(8,128)S(1)} custom-call(f32[1,128,128]{2,1,0:T(8,128)S(1)} %get-tuple-element.20), custom_call_target="InvertDiagBlocksLowerTriangular" | custom-call | tf_op jit(solution)/shard_map/jit(cholesky)/cholesky | solution.py:45
  613.0 11.7 %cholesky.132 = f32[128,128]{1,0:T(8,128)S(1)} custom-call(f32[128,128]{1,0:T(8,128)S(1)} %convolution_subtract_fusion), custom_call_target="Cholesky" | custom-call | tf_op jit(solution)/shard_map/jit(cholesky)/cholesky | solution.py:45
  624.7 0.7 compare_reduce_fusion.6
  626.8 0.8 copy.52
  (51 shorter events, 5.2 us)
Async XLA Ops:
  7.2 227.2 %copy-start = (f32[256,32]{0,1:T(8,128)S(1)}, f32[256,32]{0,1:T(8,128)}, u32[]{:S(2)}) copy-start(f32[256,32]{0,1:T(8,128)} %param.6) | copy-start | bytes 98308
  7.2 165.2 %all-reduce.5.cloned.1.call-start = ((), (), s32[]{:S(2)}) async-start(), calls=%async_computation.1 | async-start | bytes 524288 | tf_op jit(solution)/shard_map/psum | solution.py:31
  25.0 209.4 %all-reduce.7.cloned.1.call-start = ((), (), s32[]{:S(2)}) async-start(), calls=%async_computation.2 | async-start | bytes 524288 | tf_op jit(solution)/shard_map/psum | solution.py:31
  172.4 416.4 %all-reduce.9.cloned.1.call-start = ((), (), s32[]{:S(2)}) async-start(), calls=%async_computation.3 | async-start | bytes 524288 | tf_op jit(solution)/shard_map/psum | solution.py:43
  281.5 16.1 %copy-start.2 = (f32[256,32]{0,1:T(8,128)}, f32[256,32]{0,1:T(8,128)S(1)}, u32[]{:S(2)}) copy-start(f32[256,32]{0,1:T(8,128)S(1)} %convolution_bitcast_fusion.2) | copy-start | bytes 98308
  297.5 34.5 %copy-start.1 = (f32[32,16,512]{2,1,0:T(8,128)}, f32[32,16,512]{2,1,0:T(8,128)S(1)}, u32[]{:S(2)}) copy-start(f32[32,16,512]{2,1,0:T(8,128)S(1)} %reshape.41) | copy-start | bytes 3145732
Sparse Core Ops, SparseCore 0:
  25.2 147.1 all-reduce.4
  174.7 59.6 all-reduce.6
  338.1 250.6 all-reduce.8
